TPU v7x, 256 devices: a whole 4x4x8 slice. The times are simulated.
256 devices in a mesh: depth: 16 (over z, x_lo), row: 4 (over y), col: 4 (over x_hi, core).
Axes of the slice: x: 4 (x_hi: 2, x_lo: 2; x = x_hi * 2 + x_lo), y: 4, z: 8, core: 2. Of those that a mesh axis runs over, the one named last changes fastest.
Arguments:
- layer_input: bfloat16 [8192, 4096], P(('depth', 'col'), 'row'), may hold values from -6 to 6
- out_grad: bfloat16 [8192, 4096], P(('depth', 'col'), 'row'), may hold values from -6 to 6
- gate_pre: bfloat16 [8192, 14336], P(('depth', 'row'), 'col'), may hold values from -6 to 6
- up_pre: bfloat16 [8192, 14336], P(('depth', 'row'), 'col'), may hold values from -6 to 6
- gate_weight: bfloat16 [4096, 14336], P('row', 'col'), may hold values from -0.09375 to 0.09375
- up_weight: bfloat16 [4096, 14336], P('row', 'col'), may hold values from -0.09375 to 0.09375
- down_weight: bfloat16 [14336, 4096], P('col', 'row'), may hold values from -0.046875 to 0.046875
- gate_first: bfloat16 [4096, 14336], P(('row', 'depth'), 'col'), may hold values from -18 to 18
- gate_second: bfloat16 [4096, 14336], P(('row', 'depth'), 'col'), may hold values from 1 to 100
- up_first: bfloat16 [4096, 14336], P(('row', 'depth'), 'col'), may hold values from -18 to 18
- up_second: bfloat16 [4096, 14336], P(('row', 'depth'), 'col'), may hold values from 1 to 100
- down_first: bfloat16 [14336, 4096], P(('col', 'depth'), 'row'), may hold values from -18 to 18
- down_second: bfloat16 [14336, 4096], P(('col', 'depth'), 'row'), may hold values from 1 to 100
Outputs:
- input_grad: bfloat16 [8192, 4096], P(('depth', 'col'), 'row')
- new_gate: bfloat16 [4096, 14336], P(('row', 'depth'), 'col')
- new_gate_first: bfloat16 [4096, 14336], P(('row', 'depth'), 'col')
- new_gate_second: bfloat16 [4096, 14336], P(('row', 'depth'), 'col')
- new_up: bfloat16 [4096, 14336], P(('row', 'depth'), 'col')
- new_up_first: bfloat16 [4096, 14336], P(('row', 'depth'), 'col')
- new_up_second: bfloat16 [4096, 14336], P(('row', 'depth'), 'col')
- new_down: bfloat16 [14336, 4096], P(('col', 'depth'), 'row')
- new_down_first: bfloat16 [14336, 4096], P(('col', 'depth'), 'row')
- new_down_second: bfloat16 [14336, 4096], P(('col', 'depth'), 'row')
All inputs are finite; a program needn't handle non-finite values.
Results may differ from a plain program's by a relative error of at most 0.0052.
Values may be sent and summed in bfloat16 or wider, within the bound.
A program may use at most 256 MiB of HBM per device.

v0:
```python
import jax
import jax.numpy as jnp
from jax import lax
from jax.sharding import PartitionSpec as P

lr_rate = 0.0003
beta_one = 0.9
beta_two = 0.95
decay_rate = 0.1
eps_value = 1e-08
correct_one = 1.0 - 0.9**20
correct_two = 1.0 - 0.95**20


def swiglu_back(gate_pre, up_pre, hidden_grad):
    gate_val = gate_pre.astype(jnp.float32)
    up_val = up_pre.astype(jnp.float32)
    sig = jax.nn.sigmoid(gate_val)
    active = gate_val * sig
    hidden = (active * up_val).astype(jnp.bfloat16)
    gate_grad = (hidden_grad * up_val * sig * (1.0 + gate_val * (1.0 - sig))).astype(jnp.bfloat16)
    up_grad = (hidden_grad * active).astype(jnp.bfloat16)
    return (hidden, gate_grad, up_grad)


def adamw(weight, first, second, grad):
    first_new = beta_one * first.astype(jnp.float32) + (1.0 - beta_one) * grad
    second_new = beta_two * second.astype(jnp.float32) + (1.0 - beta_two) * grad * grad
    wval = weight.astype(jnp.float32)
    step_val = (
        first_new / correct_one / (jnp.sqrt(second_new / correct_two) + eps_value)
        + decay_rate * wval
    )
    new_weight = (wval - lr_rate * step_val).astype(jnp.bfloat16)
    return (new_weight, first_new.astype(jnp.bfloat16), second_new.astype(jnp.bfloat16))


def contract(left, right, left_dim, right_dim):
    return lax.dot_general(
        left, right, (((left_dim,), (right_dim,)), ((), ())), preferred_element_type=jnp.float32
    )


def on_device(
    layer_input,
    out_grad,
    gate_pre,
    up_pre,
    gate_weight,
    up_weight,
    down_weight,
    gate_first,
    gate_second,
    up_first,
    up_second,
    down_first,
    down_second,
):
    inputs_all, grads_all = (
        lax.all_gather(layer_input, "col", axis=0, tiled=True),
        lax.all_gather(out_grad, "col", axis=0, tiled=True),
    )
    hidden_grad = lax.psum_scatter(
        contract(grads_all, down_weight, 1, 1), "row", scatter_dimension=0, tiled=True
    )
    hidden, gate_grad, up_grad = swiglu_back(gate_pre, up_pre, hidden_grad)
    hidden_all, gate_all, up_all = (
        lax.all_gather(hidden, "row", axis=0, tiled=True),
        lax.all_gather(gate_grad, "row", axis=0, tiled=True),
        lax.all_gather(up_grad, "row", axis=0, tiled=True),
    )
    input_grad = lax.psum_scatter(
        contract(gate_all, gate_weight, 1, 1) + contract(up_all, up_weight, 1, 1),
        "col",
        scatter_dimension=0,
        tiled=True,
    ).astype(jnp.bfloat16)
    width_half = gate_first.shape[0]
    unit_half = down_first.shape[0]
    units = gate_weight.shape[1]
    owner = lax.axis_index("depth")
    cols = inputs_all
    both_grads = lax.psum_scatter(
        jnp.concatenate([contract(cols, gate_all, 0, 0), contract(cols, up_all, 0, 0)], axis=1),
        "depth",
        scatter_dimension=0,
        tiled=True,
    )
    grad_gate = both_grads[:, :units]
    grad_up = both_grads[:, units:]
    cols = hidden_all
    grad_down = lax.psum_scatter(
        contract(cols, grads_all, 0, 0), "depth", scatter_dimension=0, tiled=True
    )
    gate_own = lax.dynamic_slice_in_dim(gate_weight, owner * width_half, width_half, 0)
    up_own = lax.dynamic_slice_in_dim(up_weight, owner * width_half, width_half, 0)
    down_own = lax.dynamic_slice_in_dim(down_weight, owner * unit_half, unit_half, 0)
    new_gate, gate_m, gate_v = adamw(gate_own, gate_first, gate_second, grad_gate)
    new_up, up_m, up_v = adamw(up_own, up_first, up_second, grad_up)
    new_down, down_m, down_v = adamw(down_own, down_first, down_second, grad_down)
    return (input_grad, new_gate, gate_m, gate_v, new_up, up_m, up_v, new_down, down_m, down_v)


def solution(mesh):
    placed = (
        P(("depth", "col"), "row"),
        P(("depth", "col"), "row"),
        P(("depth", "row"), "col"),
        P(("depth", "row"), "col"),
        P("row", "col"),
        P("row", "col"),
        P("col", "row"),
        P(("row", "depth"), "col"),
        P(("row", "depth"), "col"),
        P(("row", "depth"), "col"),
        P(("row", "depth"), "col"),
        P(("col", "depth"), "row"),
        P(("col", "depth"), "row"),
    )
    return jax.shard_map(
        on_device,
        mesh=mesh,
        in_specs=placed,
        out_specs=(
            P(("depth", "col"), "row"),
            P(("row", "depth"), "col"),
            P(("row", "depth"), "col"),
            P(("row", "depth"), "col"),
            P(("row", "depth"), "col"),
            P(("row", "depth"), "col"),
            P(("row", "depth"), "col"),
            P(("col", "depth"), "row"),
            P(("col", "depth"), "row"),
            P(("col", "depth"), "row"),
        ),
        check_vma=False,
    )
```

profile of v0, /device:TPU:1, one launch (start us, length us, event | category | flops | bytes accessed | tf_op | source)
XLA Modules:
  0.0 1271.6 jit_solution(3392363093986072634)
XLA Ops:
  7.2 0.0 all-gather.6.cloned.1.call-start
  7.2 0.7 all-gather.6.cloned.1.call-update
  7.9 0.0 reduce-scatter.7.cloned.1.call-start
  8.0 29.4 %all-gather.6.cloned.1.call-done = bf16[512,1024]{1,0:T(8,128)(2,1)} async-done(((bf16[128,1024]{1,0:T(8,128)(2,1)}), bf16[512,1024]{1,0:T(8,128)(2,1)}) %all-gather.6.cloned.1.call-update) | async-done | bytes 1048592 | tf_op jit(solution)/shard_map/all_gather | solution.py:61
  37.4 10.3 fusion.26
  47.7 0.0 reduce-scatter.7.cloned.1.call-update
  47.7 0.0 all-gather.8.cloned.1.call-start
  47.8 74.3 %reduce-scatter.7.cloned.1.call-done = f32[128,3584]{1,0:T(8,128)} async-done(((f32[512,3584]{1,0:T(8,128)}), f32[128,3584]{1,0:T(8,128)}) %reduce-scatter.7.cloned.1.call-update) | async-done | bytes 1835024 | tf_op jit(solution)/shard_map/reduce_scatter | solution.py:63
  122.1 0.0 copy-done
  122.1 0.0 copy-done.1
  122.1 3.9 multiply_convert_fusion
  126.1 0.0 all-gather.8.cloned.1.call-update
  126.1 0.0 all-gather.10.cloned.1.call-start
  126.1 0.5 all-gather.10.cloned.1.call-update
  126.7 0.0 all-gather.14.cloned.1.call-start
  126.7 0.5 all-gather.14.cloned.1.call-update
  127.2 0.0 all-gather.12.cloned.1.call-start
  127.3 0.5 all-gather.12.cloned.1.call-update
  127.8 0.0 reduce-scatter.9.cloned.1.call-start
  127.9 44.5 %all-gather.8.cloned.1.call-done = bf16[512,3584]{1,0:T(8,128)(2,1)} async-done(((bf16[128,3584]{1,0:T(8,128)(2,1)}), bf16[512,3584]{1,0:T(8,128)(2,1)}) %all-gather.8.cloned.1.call-update) | async-done | bytes 3670032 | tf_op jit(solution)/shard_map/all_gather | solution.py:69
  172.4 7.4 fusion.27
  179.8 0.0 copy-start.9
  179.8 41.1 %all-gather.10.cloned.1.call-done = bf16[512,3584]{1,0:T(8,128)(2,1)} async-done(((bf16[128,3584]{1,0:T(8,128)(2,1)}), bf16[512,3584]{1,0:T(8,128)(2,1)}) %all-gather.10.cloned.1.call-update) | async-done | bytes 3670032 | tf_op jit(solution)/shard_map/all_gather | solution.py:70
  220.8 9.5 convolution_add_fusion
  230.4 0.0 reduce-scatter.9.cloned.1.call-update
  230.4 0.0 reduce-scatter.11.cloned.1.call-start
  230.5 38.8 %all-gather.14.cloned.1.call-done = bf16[512,3584]{1,0:T(8,128)(2,1)} async-done(((bf16[128,3584]{1,0:T(8,128)(2,1)}), bf16[512,3584]{1,0:T(8,128)(2,1)}) %all-gather.14.cloned.1.call-update) | async-done | bytes 3670032 | tf_op jit(solution)/shard_map/all_gather | solution.py:68
  269.3 9.4 fusion.28
  278.7 0.0 reduce-scatter.11.cloned.1.call-update
  278.7 0.2 reduce-scatter.13.cloned.1.call-start
  278.9 16.0 %all-gather.12.cloned.1.call-done = bf16[512,1024]{1,0:T(8,128)(2,1)} async-done(((bf16[128,1024]{1,0:T(8,128)(2,1)}), bf16[512,1024]{1,0:T(8,128)(2,1)}) %all-gather.12.cloned.1.call-update) | async-done | bytes 1048592 | tf_op jit(solution)/shard_map/all_gather | solution.py:60
  295.0 6.6 convolution_bitcast_fusion
  301.6 4.0 convolution_bitcast_fusion.1
  305.6 16.4 %pad_maximum_fusion = f32[1024,7168]{0,1:T(8,128)} fusion(f32[1024,3584]{0,1:T(8,128)S(1)} %convolution_bitcast_fusion, f32[1024,3584]{0,1:T(8,128)S(1)} %convolution_bitcast_fusion.1), kind=kLoop, calls=%fused_computation | loop fusion | flops 7340032 | bytes 58720256 | tf_op jit(solution)/shard_map/concatenate | solution.py:84
  322.0 29.7 %copy.49 = f32[1024,7168]{1,0:T(8,128)} copy(f32[1024,7168]{0,1:T(8,128)} %pad_maximum_fusion) | data formatting | bytes 58720256
  351.7 0.0 reduce-scatter.13.cloned.1.call-update
  351.8 0.0 copy-start.4
  351.8 0.0 copy-start.5
  351.8 0.0 copy-start.6
  351.8 0.0 copy-start.7
  351.8 0.0 reduce-scatter.9.cloned.1.call-done
  351.9 1.9 convert_element_type.76
  353.8 298.1 %reduce-scatter.11.cloned.1.call-done = f32[224,1024]{1,0:T(8,128)} async-done(((f32[3584,1024]{1,0:T(8,128)}), f32[224,1024]{1,0:T(8,128)}) %reduce-scatter.11.cloned.1.call-update) | async-done | bytes 917520 | tf_op jit(solution)/shard_map/reduce_scatter | solution.py:92
  651.9 3.4 fusion.23
  655.3 604.9 %reduce-scatter.13.cloned.1.call-done = f32[64,7168]{1,0:T(8,128)} async-done(((f32[1024,7168]{1,0:T(8,128)}), f32[64,7168]{1,0:T(8,128)}) %reduce-scatter.13.cloned.1.call-update) | async-done | bytes 1835024 | tf_op jit(solution)/shard_map/reduce_scatter | solution.py:83
  1260.2 0.0 copy-done.5
  1260.2 0.0 copy-done.7
  1260.2 4.8 fusion.24
  (13 shorter events, 0.0 us)
Async XLA Ops:
  7.2 30.2 %all-gather.6.cloned.1.call-start = ((), (), s32[]{:S(2)}) async-start(), calls=%async_computation.4 | async-start | bytes 1310720 | tf_op jit(solution)/shard_map/all_gather | solution.py:61
  7.9 114.2 %reduce-scatter.7.cloned.1.call-start = ((), (), s32[]{:S(2)}) async-start(), calls=%async_computation.5 | async-start | bytes 9175040 | tf_op jit(solution)/shard_map/reduce_scatter | solution.py:63
  47.7 74.4 %copy-start = (bf16[128,3584]{1,0:T(8,128)(2,1)S(1)}, bf16[128,3584]{1,0:T(8,128)(2,1)}, u32[]{:S(2)}) copy-start(bf16[128,3584]{1,0:T(8,128)(2,1)} %param.15) | copy-start | bytes 2752516
  47.7 74.4 %copy-start.1 = (bf16[128,3584]{1,0:T(8,128)(2,1)S(1)}, bf16[128,3584]{1,0:T(8,128)(2,1)}, u32[]{:S(2)}) copy-start(bf16[128,3584]{1,0:T(8,128)(2,1)} %param.16) | copy-start | bytes 2752516
  47.7 124.6 %all-gather.8.cloned.1.call-start = ((), (), s32[]{:S(2)}) async-start(), calls=%async_computation.6 | async-start | bytes 4587520 | tf_op jit(solution)/shard_map/all_gather | solution.py:69
  126.1 94.8 %all-gather.10.cloned.1.call-start = ((), (), s32[]{:S(2)}) async-start(), calls=%async_computation.7 | async-start | bytes 4587520 | tf_op jit(solution)/shard_map/all_gather | solution.py:70
  126.7 142.6 %all-gather.14.cloned.1.call-start = ((), (), s32[]{:S(2)}) async-start(), calls=%async_computation.10 | async-start | bytes 4587520 | tf_op jit(solution)/shard_map/all_gather | solution.py:68
  127.2 167.7 %all-gather.12.cloned.1.call-start = ((), (), s32[]{:S(2)}) async-start(), calls=%async_computation.9 | async-start | bytes 1310720 | tf_op jit(solution)/shard_map/all_gather | solution.py:60
  127.8 224.0 %reduce-scatter.9.cloned.1.call-start = ((), (), s32[]{:S(2)}) async-start(), calls=%async_computation.8 | async-start | bytes 2621440 | tf_op jit(solution)/shard_map/reduce_scatter | solution.py:72
  179.8 89.5 %copy-start.9 = (bf16[512,1024]{1,0:T(8,128)(2,1)S(1)}, bf16[512,1024]{1,0:T(8,128)(2,1)}, u32[]{:S(2)}) copy-start(bf16[512,1024]{1,0:T(8,128)(2,1)} %all-gather.6.cloned.1.call-done) | copy-start | bytes 3145732
  230.4 421.4 %reduce-scatter.11.cloned.1.call-start = ((), (), s32[]{:S(2)}) async-start(), calls=%async_computation.11 | async-start | bytes 15597568 | tf_op jit(solution)/shard_map/reduce_scatter | solution.py:92
  278.7 981.5 %reduce-scatter.13.cloned.1.call-start = ((), (), s32[]{:S(2)}) async-start(), calls=%async_computation.12 | async-start | bytes 31195136 | tf_op jit(solution)/shard_map/reduce_scatter | solution.py:83
  295.0 6.6 copy-start.8
  295.0 6.6 copy-start.10
  351.7 300.1 %copy-start.2 = (bf16[224,1024]{1,0:T(8,128)(2,1)S(1)}, bf16[224,1024]{1,0:T(8,128)(2,1)}, u32[]{:S(2)}) copy-start(bf16[224,1024]{1,0:T(8,128)(2,1)} %param.25) | copy-start | bytes 1376260
  351.7 300.1 %copy-start.3 = (bf16[224,1024]{1,0:T(8,128)(2,1)S(1)}, bf16[224,1024]{1,0:T(8,128)(2,1)}, u32[]{:S(2)}) copy-start(bf16[224,1024]{1,0:T(8,128)(2,1)} %param.24) | copy-start | bytes 1376260
  351.8 908.5 %copy-start.4 = (bf16[64,3584]{1,0:T(8,128)(2,1)S(1)}, bf16[64,3584]{1,0:T(8,128)(2,1)}, u32[]{:S(2)}) copy-start(bf16[64,3584]{1,0:T(8,128)(2,1)} %param.23) | copy-start | bytes 1376260
  351.8 908.4 %copy-start.5 = (bf16[64,3584]{1,0:T(8,128)(2,1)S(1)}, bf16[64,3584]{1,0:T(8,128)(2,1)}, u32[]{:S(2)}) copy-start(bf16[64,3584]{1,0:T(8,128)(2,1)} %param.22) | copy-start | bytes 1376260
  351.8 908.4 %copy-start.6 = (bf16[64,3584]{1,0:T(8,128)(2,1)S(1)}, bf16[64,3584]{1,0:T(8,128)(2,1)}, u32[]{:S(2)}) copy-start(bf16[64,3584]{1,0:T(8,128)(2,1)} %param.20) | copy-start | bytes 1376260
  351.8 908.4 %copy-start.7 = (bf16[64,3584]{1,0:T(8,128)(2,1)S(1)}, bf16[64,3584]{1,0:T(8,128)(2,1)}, u32[]{:S(2)}) copy-start(bf16[64,3584]{1,0:T(8,128)(2,1)} %param.21) | copy-start | bytes 1376260
Sparse Core Ops, SparseCore 0:
  9.8 27.4 all-gather.5
  47.9 74.2 reduce-scatter.6
  126.2 46.1 all-gather.7
  174.1 46.7 all-gather.9
  222.5 46.7 all-gather.13
  271.0 23.9 all-gather.11
  297.7 42.5 reduce-scatter.8
  343.0 308.7 reduce-scatter.10
  654.6 605.5 reduce-scatter.12
where the time goes:
time: 1270 us
  waiting for transfers between devices  1150 us (91%)
  matrix products  47.3 us (4%)
  other arithmetic  30.5 us (2%)
  local copies, waits for them, and re-layouts  29.8 us (2%)
  between operations  14 us (1%)
    reduce_scatter x1, waiting for transfers between devices, on_device(): lax.psum_scatter(jnp.concatenate([contract(cols, gate_all, 0, 0), contrac...  605 us
    reduce_scatter x1, waiting for transfers between devices, on_device(): lax.psum_scatter(contract(cols, grads_all, 0, 0), 'depth', scatter_dimens...  298 us
    reduce_scatter x1, waiting for transfers between devices, on_device(): lax.psum_scatter(contract(grads_all, down_weight, 1, 1), 'row', scatter_d...  74.3 us
    dot_general x6, matrix products, contract(): lax.dot_general(left, right, (((left_dim,), (right_dim,)), ((), ())), pre...  47.3 us
    all_gather x1, waiting for transfers between devices, on_device(): lax.all_gather(gate_grad, 'row', axis=0, tiled=True)  44.5 us
    all_gather x1, waiting for transfers between devices, on_device(): lax.all_gather(up_grad, 'row', axis=0, tiled=True)  41.1 us
    all_gather x1, waiting for transfers between devices, on_device(): lax.all_gather(hidden, 'row', axis=0, tiled=True)  38.8 us
    unnamed x23, local copies, waits for them, and re-layouts  29.8 us
  transfers between devices with their start and end apart: 9, of which 8 were waited for; matrix products, arithmetic and copies ran while one was open for 7% of the time, Pallas kernels for 0%

commit v1 on v0

v1 whole, which is shorter than its diff:
```python
import jax
import jax.numpy as jnp
from jax import lax
from jax.experimental import pallas as pl
from jax.experimental.pallas import tpu as pltpu
from jax.sharding import PartitionSpec as P

BF = jnp.bfloat16
F32 = jnp.float32
MESH = pl.DeviceIdType.MESH

lr_rate = 0.0003
beta_one = 0.9
beta_two = 0.95
decay_rate = 0.1
eps_value = 1e-08
correct_one = 1.0 - 0.9**20
correct_two = 1.0 - 0.95**20

NZ = 8
CB = 512
NB = 7
NQ = 2 * NB
ZR = 128
UR = 448
DK = 4
DC = 256


def adamw(weight, first, second, grad):
    first_new = beta_one * first.astype(F32) + (1.0 - beta_one) * grad
    second_new = beta_two * second.astype(F32) + (1.0 - beta_two) * grad * grad
    wval = weight.astype(F32)
    step_val = (
        first_new / correct_one / (jnp.sqrt(second_new / correct_two) + eps_value)
        + decay_rate * wval
    )
    return (
        (wval - lr_rate * step_val).astype(BF),
        first_new.astype(BF),
        second_new.astype(BF),
    )


def dot_nn(a, b):
    return lax.dot_general(a, b, (((1,), (0,)), ((), ())), preferred_element_type=F32)


def dot_nt(a, b):
    return lax.dot_general(a, b, (((1,), (1,)), ((), ())), preferred_element_type=F32)


def rows_of(index, size):
    return pl.ds(pl.multiple_of(index * size, size), size)


def kernel(
    x_ref, do_ref, gp_ref, up_ref, wg, wu, wd, gm, gv, um, uv, dm, dv,
    ig_out, ng, ngm, ngv, nu, num, nuv, nd, ndm, ndv,
    do_all, xt_all, ht_all, gu, wdb, wgb, a_s, a_own, a_r,
    s0, rl, rs, fin, acc, xs, xr, abuf,
    s0d, rld, rsd, find, accd, xsd, xrd, dab,
    igacc, igs, igr, igo,
    do_ss, do_rs, xt_ss, xt_rs, ht_ss, ht_rs, a_ss, a_rs, b_ss, b_rs,
    l_ss, l_rs, h_ss, h_rs, x_ss, x_rs,
    dl_ss, dl_rs, dh_ss, dh_rs, dx_ss, dx_rs,
    ig_ss, ig_rs, wd_sem, wg_sem, ab_sem, ob_sem, da_sem, igo_sem,
):
    d = lax.axis_index("depth")
    r = lax.axis_index("row")
    c = lax.axis_index("col")
    z = lax.div(d, 2)
    xl = lax.rem(d, 2)

    def zmod(v):
        return lax.rem(v + 16, NZ)

    def zdev(v):
        return (2 * zmod(v) + xl, r, c)

    xdev = (2 * z + 1 - xl, r, c)

    def ydev(k):
        return (d, lax.rem(r + k, 4), c)

    def cdev(k):
        return (d, r, lax.rem(c + k, 4))

    def rc(src, dst, ss, rsem, dev):
        return pltpu.make_async_remote_copy(
            src_ref=src, dst_ref=dst, send_sem=ss, recv_sem=rsem,
            device_id=dev, device_id_type=MESH,
        )

    def lc(src, dst, sem):
        return pltpu.make_async_copy(src, dst, sem)

    def wd_copy(j, par):
        return lc(wd.at[rows_of(j, CB), :], wdb.at[par], wd_sem.at[par])

    def wg_start(q, par):
        cols = rows_of(lax.div(q, 2), CB)

        @pl.when(par == 0)
        def _():
            lc(wg.at[:, cols], wgb.at[0], wg_sem.at[0]).start()

        @pl.when(par == 1)
        def _():
            lc(wu.at[:, cols], wgb.at[1], wg_sem.at[1]).start()

    for p in range(2):
        wd_copy(p, p).start()
    lc(wg.at[:, pl.ds(0, CB)], wgb.at[0], wg_sem.at[0]).start()
    lc(wu.at[:, pl.ds(0, CB)], wgb.at[1], wg_sem.at[1]).start()
    lc(wd.at[rows_of(d, 224), :], dab.at[0], da_sem.at[0]).start()
    lc(dm, dab.at[1], da_sem.at[1]).start()
    lc(dv, dab.at[2], da_sem.at[2]).start()

    barrier = pltpu.get_barrier_semaphore()
    partners = [zdev(z + 1), zdev(z - 1), xdev]
    partners += [ydev(k) for k in (1, 2, 3)] + [cdev(k) for k in (1, 2, 3)]
    for dev in partners:
        pl.semaphore_signal(barrier, inc=1, device_id=dev, device_id_type=MESH)
    pl.semaphore_wait(barrier, len(partners))

    own_c = rows_of(c, 128)
    own_r = rows_of(r, 128)

    def do_copy(k):
        return rc(do_ref, do_all.at[own_c, :], do_ss.at[k - 1], do_rs.at[k - 1], cdev(k))

    for k in (2, 1, 3):
        do_copy(k).start()
    do_all[own_c, :] = do_ref[...]

    @pl.loop(0, NB)
    def _(j):
        cols = rows_of(j, CB)
        g = gp_ref[:, cols].astype(F32)
        h = g * jax.nn.sigmoid(g) * up_ref[:, cols].astype(F32)
        ht_all[cols, own_r] = h.T.astype(BF)

    def ht_copy(i, k):
        away = (2 * lax.rem(i, 2) - 1) * (4 - lax.div(i + 1, 2))
        view = ht_all.at[rows_of(zmod(z + away), UR), own_r]
        return rc(view, view, ht_ss.at[i, k - 1], ht_rs.at[i, k - 1], ydev(k))

    @pl.loop(0, NZ)
    def _(i):
        for k in (2, 1, 3):
            ht_copy(i, k).start()

    xt_all[:, own_c] = x_ref[...].T

    def xt_copy(k):
        view = xt_all.at[:, own_c]
        return rc(view, view, xt_ss.at[k - 1], xt_rs.at[k - 1], cdev(k))

    for k in (2, 1, 3):
        xt_copy(k).start()

    def a_copy(j, par, k):
        return rc(a_s.at[par, k - 1], a_r.at[j, k - 1], a_ss.at[par, k - 1],
                  a_rs.at[j, k - 1], ydev(k))

    def stage_a(j):
        par = lax.rem(j, 2)
        wd_copy(j, par).wait()

        @pl.when(j >= 2)
        def _():
            for k in (2, 1, 3):
                a_copy(j, par, k).wait_send()

        def part(k):
            return dot_nt(do_all[rows_of(lax.rem(r + k, 4), 128), :], wdb[par])

        for k in (2, 1, 3):
            a_s[par, k - 1] = part(k).astype(BF)
            a_copy(j, par, k).start()
        a_own[par] = part(0)

        @pl.when(j + 2 < NB)
        def _():
            wd_copy(j + 2, par).start()

    def b_copy(q, k):
        view = gu.at[q, own_r, :]
        return rc(view, view, b_ss.at[q, k - 1], b_rs.at[q, k - 1], ydev(k))

    def stage_b(j):
        par = lax.rem(j, 2)
        for k in (2, 1, 3):
            a_copy(j, par, k).wait_recv()

        @pl.loop(0, 8)
        def _(i):
            sub = rows_of(i, 16)
            cols = rows_of(j, CB)
            hg = a_own[par, sub, :]
            for k in range(3):
                hg += a_r[j, k, sub, :].astype(F32)
            g = gp_ref[sub, cols].astype(F32)
            u = up_ref[sub, cols].astype(F32)
            sig = jax.nn.sigmoid(g)
            dst = pl.ds(pl.multiple_of(r * 128 + i * 16, 16), 16)
            gu[2 * j, dst, :] = (hg * u * sig * (1.0 + g * (1.0 - sig))).astype(BF)
            gu[2 * j + 1, dst, :] = (hg * (g * sig)).astype(BF)

        for t in range(2):
            for k in (2, 1, 3):
                b_copy(2 * j + t, k).start()

    def ring(step, job, par, sign, first, slots, ssem, rsem, hops, dot):
        dest = zmod(z + sign * (hops - step))
        val = dot(dest)
        if step == 0:
            src = first.at[par]
        else:
            src = slots.at[job, step - 1]
            prev = first.at[par] if step == 1 else slots.at[job, step - 2]
            rc(prev, src, ssem.at[par, step - 1], rsem.at[job, step - 1], zdev(z + sign)).wait()
            val += src[...].astype(F32)
        src[...] = val.astype(BF)
        rc(src, slots.at[job, step], ssem.at[par, step], rsem.at[job, step],
           zdev(z + sign)).start()

    def ring_end(job, par, sign, slots_l, slots_h, lss, lrs, hss, hrs, dot):
        val = dot(z)
        last = slots_l.at[job, 3]
        rc(slots_l.at[job, 2], last, lss.at[par, 3], lrs.at[job, 3], zdev(z + sign)).wait()
        val += last[...].astype(F32)
        last = slots_h.at[job, 2]
        rc(slots_h.at[job, 1], last, hss.at[par, 2], hrs.at[job, 2], zdev(z - sign)).wait()
        return val + last[...].astype(F32)

    def down_dot(k):
        def dot(dest):
            return dot_nn(ht_all[rows_of(dest, UR), :], do_all[:, rows_of(k, DC)])
        return dot

    own_u = rows_of(xl, 224)
    other_u = rows_of(1 - xl, 224)

    def dx_copy(k):
        return rc(xsd.at[k], xrd.at[k], dx_ss.at[k], dx_rs.at[k], xdev)

    def down_step(step):
        @pl.loop(0, DK)
        def _(k):
            sign = 1 - 2 * lax.rem(k, 2)
            ring(step, k, k, sign, s0d.at[0], rld, dl_ss, dl_rs, 4, down_dot(k))
            if step < 3:
                ring(step, k, k, -sign, s0d.at[1], rsd, dh_ss, dh_rs, 3, down_dot(k))

    def down_end():
        @pl.loop(0, DK)
        def _(k):
            sign = 1 - 2 * lax.rem(k, 2)
            find[...] = ring_end(k, k, sign, rld, rsd, dl_ss, dl_rs, dh_ss, dh_rs, down_dot(k))
            accd[k] = find[own_u, :]
            xsd[k] = find[other_u, :].astype(BF)
            dx_copy(k).start()

    def da_out(i):
        return lc(dab.at[i], (nd, ndm, ndv)[i], da_sem.at[i])

    def down_update():
        lc(wd.at[rows_of(d, 224), :], dab.at[0], da_sem.at[0]).wait()
        lc(dm, dab.at[1], da_sem.at[1]).wait()
        lc(dv, dab.at[2], da_sem.at[2]).wait()

        @pl.loop(0, DK)
        def _(k):
            dx_copy(k).wait()
            cols = rows_of(k, DC)

            @pl.loop(0, 7)
            def _(i):
                sub = rows_of(i, 32)
                grad = accd[k, sub, :] + xrd[k, sub, :].astype(F32)
                new = adamw(dab[0, sub, cols], dab[1, sub, cols], dab[2, sub, cols], grad)
                for n in range(3):
                    dab[n, sub, cols] = new[n]

        for i in range(3):
            da_out(i).start()

    def gu_dot(q):
        def dot(dest):
            return dot_nn(xt_all[rows_of(dest, ZR), :], gu[q])
        return dot

    own_w = rows_of(xl, 64)
    other_w = rows_of(1 - xl, 64)

    def x_copy(q):
        par = lax.rem(q, 2)
        return rc(xs.at[par], xr.at[q], x_ss.at[par], x_rs.at[q], xdev)

    def ab_copies(q, par, out):
        cols = rows_of(lax.div(q, 2), CB)
        for t in range(2):
            refs = ((ng, ngm, ngv), (nu, num, nuv))[t] if out else ((wg, gm, gv), (wu, um, uv))[t]

            @pl.when(par == t)
            def _():
                for n in range(3):
                    if out:
                        lc(abuf.at[t, n], refs[n].at[:, cols], ob_sem.at[t, n]).start()
                    elif n == 0:
                        lc(refs[0].at[rows_of(d, 64), cols], abuf.at[t, n], ab_sem.at[t, n]).start()
                    else:
                        lc(refs[n].at[:, cols], abuf.at[t, n], ab_sem.at[t, n]).start()

    def ob_wait(par):
        for n in range(3):
            lc(abuf.at[par, n], ng.at[:, pl.ds(0, CB)], ob_sem.at[par, n]).wait()

    def gu_step(step, q):
        par = lax.rem(q, 2)
        sign = 1 - 2 * par
        ring(step, q, par, sign, s0.at[0], rl, l_ss, l_rs, 4, gu_dot(q))
        if step < 3:
            ring(step, q, par, -sign, s0.at[1], rs, h_ss, h_rs, 3, gu_dot(q))

    def gu_end(q):
        par = lax.rem(q, 2)

        @pl.when(q >= 2)
        def _():
            ob_wait(par)

        ab_copies(q, par, False)
        sign = 1 - 2 * par
        fin[...] = ring_end(q, par, sign, rl, rs, l_ss, l_rs, h_ss, h_rs, gu_dot(q))
        xs[par] = fin[other_w, :].astype(BF)
        x_copy(q).start()
        acc[par] = fin[own_w, :]

    def gu_update(q):
        par = lax.rem(q, 2)
        for n in range(3):
            lc(gm.at[:, pl.ds(0, CB)], abuf.at[par, n], ab_sem.at[par, n]).wait()
        x_copy(q).wait()

        @pl.loop(0, 4)
        def _(i):
            sub = rows_of(i, 16)
            grad = acc[par, sub, :] + xr[q, sub, :].astype(F32)
            new = adamw(abuf[par, 0, sub, :], abuf[par, 1, sub, :], abuf[par, 2, sub, :], grad)
            for n in range(3):
                abuf[par, n, sub, :] = new[n]

        ab_copies(q, par, True)

    def ig_add(q):
        par = lax.rem(q, 2)
        lc(wg.at[:, pl.ds(0, CB)], wgb.at[par], wg_sem.at[par]).wait()

        @pl.loop(0, 4)
        def _(i):
            sub = rows_of(i, 128)
            val = dot_nt(gu[q, sub, :], wgb[par])

            @pl.when(q == 0)
            def _():
                igacc[sub, :] = val

            @pl.when(q > 0)
            def _():
                igacc[sub, :] += val

        @pl.when(q + 2 < NQ)
        def _():
            wg_start(q + 2, par)

    def ig_copy(k):
        return rc(igs.at[k - 1], igr.at[k - 1], ig_ss.at[k - 1], ig_rs.at[k - 1], cdev(k))

    def ig_send():
        for k in (2, 1, 3):
            igs[k - 1] = igacc[rows_of(lax.rem(c + k, 4), 128), :].astype(BF)
            ig_copy(k).start()

    def ig_end():
        for k in (2, 1, 3):
            ig_copy(k).wait()
        val = igacc[own_c, :]
        for k in range(3):
            val += igr[k].astype(F32)
        igo[...] = val.astype(BF)
        lc(igo, ig_out, igo_sem).start()

    def ht_wait(*blocks):
        for i in blocks:
            for k in (2, 1, 3):
                ht_copy(i, k).wait_recv()

    for k in (2, 1, 3):
        do_copy(k).wait()

    @pl.loop(0, 4)
    def _(i):
        stage_a(i)

        @pl.when(i >= 1)
        def _():
            stage_b(i - 1)

        for step, blocks in enumerate(((0, 1, 2), (3, 4), (5, 6), (7,))):
            @pl.when(i == step)
            def _():
                ht_wait(*blocks)
                down_step(step)

    for k in (2, 1, 3):
        xt_copy(k).wait()

    @pl.loop(0, NQ + 5)
    def _(t):
        for step in (3, 2, 1, 0):
            q = t - step

            @pl.when((q >= 0) & (q < NQ))
            def _():
                if step == 0:
                    for k in (2, 1, 3):
                        b_copy(q, k).wait_recv()
                gu_step(step, q)

        half = lax.div(t, 2)

        @pl.when((lax.rem(t, 2) == 0) & (half + 4 < NB))
        def _():
            stage_a(half + 4)

        @pl.when((lax.rem(t, 2) == 1) & (half + 3 < NB))
        def _():
            stage_b(half + 3)

        @pl.when((t >= 4) & (t - 4 < NQ))
        def _():
            gu_end(t - 4)

        @pl.when(t >= 5)
        def _():
            gu_update(t - 5)

        @pl.when(t < NQ)
        def _():
            ig_add(t)

        @pl.when(t == 1)
        def _():
            down_end()

        @pl.when(t == 2)
        def _():
            down_update()

        @pl.when(t == NQ)
        def _():
            ig_send()

        @pl.when(t == NQ + 3)
        def _():
            ig_end()

    for i in range(3):
        da_out(i).wait()
    lc(igo, ig_out, igo_sem).wait()
    for par in range(2):
        ob_wait(par)
        for k in (2, 1, 3):
            a_copy(0, par, k).wait_send()

    @pl.loop(0, NZ)
    def _(i):
        for k in (2, 1, 3):
            ht_copy(i, k).wait_send()

    @pl.loop(0, NQ)
    def _(q):
        for k in (2, 1, 3):
            b_copy(q, k).wait_send()


def on_device(*args):
    vm = pltpu.VMEM
    dma = pltpu.SemaphoreType.DMA
    scratch = [
        vm((512, 1024), BF),
        vm((1024, 512), BF),
        vm((3584, 512), BF),
        vm((NQ, 512, CB), BF),
        vm((2, CB, 1024), BF),
        vm((2, 1024, CB), BF),
        vm((2, 3, 128, CB), BF),
        vm((2, 128, CB), F32),
        vm((NB, 3, 128, CB), BF),
        vm((2, 2, ZR, CB), BF),
        vm((NQ, 4, ZR, CB), BF),
        vm((NQ, 3, ZR, CB), BF),
        vm((ZR, CB), F32),
        vm((2, 64, CB), F32),
        vm((2, 64, CB), BF),
        vm((NQ, 64, CB), BF),
        vm((2, 3, 64, CB), BF),
        vm((2, DK, UR, DC), BF),
        vm((DK, 4, UR, DC), BF),
        vm((DK, 3, UR, DC), BF),
        vm((UR, DC), F32),
        vm((DK, 224, DC), F32),
        vm((DK, 224, DC), BF),
        vm((DK, 224, DC), BF),
        vm((3, 224, 1024), BF),
        vm((512, 1024), F32),
        vm((3, 128, 1024), BF),
        vm((3, 128, 1024), BF),
        vm((128, 1024), BF),
        dma((3,)), dma((3,)), dma((3,)), dma((3,)),
        dma((NZ, 3)), dma((NZ, 3)),
        dma((2, 3)), dma((NB, 3)),
        dma((NQ, 3)), dma((NQ, 3)),
        dma((2, 4)), dma((NQ, 4)),
        dma((2, 3)), dma((NQ, 3)),
        dma((2,)), dma((NQ,)),
        dma((DK, 4)), dma((DK, 4)),
        dma((DK, 3)), dma((DK, 3)),
        dma((DK,)), dma((DK,)),
        dma((3,)), dma((3,)),
        dma((2,)), dma((2,)), dma((2, 3)), dma((2, 3)), dma((3,)), dma(()),
    ]
    shapes = [(128, 1024)] + [(64, 3584)] * 6 + [(224, 1024)] * 3
    in_vmem = pl.BlockSpec(memory_space=pltpu.VMEM)
    in_any = pl.BlockSpec(memory_space=pl.ANY)
    return pl.pallas_call(
        kernel,
        out_shape=[jax.ShapeDtypeStruct(s, BF) for s in shapes],
        in_specs=[in_vmem] * 4 + [in_any] * 9,
        out_specs=[in_any] * 10,
        scratch_shapes=scratch,
        compiler_params=pltpu.CompilerParams(
            collective_id=0, has_side_effects=True, vmem_limit_bytes=60 * 2**20
        ),
        cost_estimate=pl.CostEstimate(
            flops=22548578304, bytes_accessed=34000000, transcendentals=4000000
        ),
    )(*args)


def solution(mesh):
    act = P(("depth", "col"), "row")
    pre = P(("depth", "row"), "col")
    wide = P("row", "col")
    tall = P("col", "row")
    wide_own = P(("row", "depth"), "col")
    tall_own = P(("col", "depth"), "row")
    return jax.shard_map(
        on_device,
        mesh=mesh,
        in_specs=(act, act, pre, pre, wide, wide, tall) + (wide_own,) * 4 + (tall_own,) * 2,
        out_specs=(act,) + (wide_own,) * 6 + (tall_own,) * 3,
        check_vma=False,
    )
```

time: 1270 us -> 281 us (0.22)
  waiting for transfers between devices: 1150 us -> 0 us
  Pallas kernels: 0 us -> 259 us
  matrix products: 47.3 us -> 0 us
  other arithmetic: 30.5 us -> 0 us
  between operations: 14 us -> 0.67 us
  local copies, waits for them, and re-layouts: 29.8 us -> 17 us
    reduce_scatter x4 -> x0, waiting for transfers between devices: 977 us -> none  [the longest x1 605 us: on_device(): lax.psum_scatter(jnp.concatenate([contract(cols, gate_all, 0, 0), contrac...]
    pallas_call x0 -> x1, Pallas kernels: none -> 259 us  [on_device(): pl.pallas_call(kernel, out_shape=[jax.ShapeDtypeStruct(s, BF) for s in sh...]
    all_gather x5 -> x0, waiting for transfers between devices: 170 us -> none  [the longest x1 44.5 us: on_device(): lax.all_gather(gate_grad, 'row', axis=0, tiled=True)]
    dot_general x6 -> x0, matrix products: 47.3 us -> none  [contract(): lax.dot_general(left, right, (((left_dim,), (right_dim,)), ((), ())), pre...]
    concatenate x1 -> x0, other arithmetic: 16.4 us -> none  [on_device(): jnp.concatenate([contract(cols, gate_all, 0, 0), contract(cols, up_all, 0...]
    convert_element_type x4 -> x0, other arithmetic: 14.1 us -> none  [the longest x2 8.24 us: adamw(): second_new.astype(jnp.bfloat16)]
    unnamed x23 -> x12, local copies, waits for them, and re-layouts: 29.8 us -> 17 us
  transfers between devices with their start and end apart: 9 -> 0, of which waited for: 8 -> 0; matrix products, arithmetic and copies ran while one was open for 7% -> 0% of each run, Pallas kernels for 0% -> 0%
where the time goes in v1:
time: 281 us; the launch traced here: 277 us
  Pallas kernels  259 us (92%)
  local copies, waits for them, and re-layouts  17 us (6%)
    pallas_call x1, Pallas kernels, on_device(): pl.pallas_call(kernel, out_shape=[jax.ShapeDtypeStruct(s, BF) for s in sh...  259 us
    unnamed x12, local copies, waits for them, and re-layouts  17 us

profile of v1, /device:TPU:1, one launch (start us, length us, event | category | flops | bytes accessed | tf_op | source)
XLA Modules:
  0.0 277.1 jit_solution(9687579108828919456)
XLA Ops:
  0.6 259.4 %shard_map.204 = (bf16[128,1024]{1,0:T(8,128)(2,1)}, bf16[64,3584]{1,0:T(8,128)(2,1)}, bf16[64,3584]{1,0:T(8,128)(2,1)}, bf16[64,3584]{1,0:T(8,128)(2,1)}, bf16[...) custom-call(bf16[128,1024]{1,0:T(8,128)(2,1)} %x_ref.1, ...), custom_call_target="tpu_custom_call" | custom-call | flops 22548578304 | bytes 34000000 | tf_op jit(solution)/shard_map/pallas_call | solution.py:539
  260.1 0.0 copy-start
  260.1 1.7 copy.33
  261.8 1.8 copy.34
  263.6 1.8 copy.35
  265.4 1.8 copy.36
  267.2 1.8 copy.37
  269.0 1.8 copy.38
  270.9 1.8 copy.39
  272.7 1.8 copy.40
  274.5 1.8 copy.41
  276.3 0.0 copy-done
  276.3 0.8 copy.42
Async XLA Ops:
  260.1 16.3 %copy-start = (bf16[224,1024]{1,0:T(8,128)(2,1)S(1)}, bf16[224,1024]{1,0:T(8,128)(2,1)}, u32[]{:S(2)}) copy-start(bf16[224,1024]{1,0:T(8,128)(2,1)} %get-tuple-element.29) | copy-start | bytes 1376260

commit v2 on v1

--- a/solution.py
+++ b/solution.py
@@ -23,7 +23,7 @@
 NQ = 2 * NB
 ZR = 128
 UR = 448
-DK = 4
+DK = 2
 DC = 256
 
 
@@ -58,12 +58,14 @@
     x_ref, do_ref, gp_ref, up_ref, wg, wu, wd, gm, gv, um, uv, dm, dv,
     ig_out, ng, ngm, ngv, nu, num, nuv, nd, ndm, ndv,
     do_all, xt_all, ht_all, gu, wdb, wgb, a_s, a_own, a_r,
-    s0, rl, rs, fin, acc, xs, xr, abuf,
-    s0d, rld, rsd, find, accd, xsd, xrd, dab,
+    s0, rl, rs, fin, acc, xs, xr, abuf, s0x, rlx, rsx, xps, xpr,
+    s0d, rld, rsd, find, accd, xsd, xrd, dab, s0dx, rldx, rsdx, xpsd, xprd,
     igacc, igs, igr, igo,
     do_ss, do_rs, xt_ss, xt_rs, ht_ss, ht_rs, a_ss, a_rs, b_ss, b_rs,
     l_ss, l_rs, h_ss, h_rs, x_ss, x_rs,
+    lx_ss, lx_rs, hx_ss, hx_rs, xp_ss, xp_rs,
     dl_ss, dl_rs, dh_ss, dh_rs, dx_ss, dx_rs,
+    dlx_ss, dlx_rs, dhx_ss, dhx_rs, dxp_ss, dxp_rs,
     ig_ss, ig_rs, wd_sem, wg_sem, ab_sem, ob_sem, da_sem, igo_sem,
 ):
     d = lax.axis_index("depth")
@@ -122,17 +124,9 @@
     partners += [ydev(k) for k in (1, 2, 3)] + [cdev(k) for k in (1, 2, 3)]
     for dev in partners:
         pl.semaphore_signal(barrier, inc=1, device_id=dev, device_id_type=MESH)
-    pl.semaphore_wait(barrier, len(partners))
 
     own_c = rows_of(c, 128)
     own_r = rows_of(r, 128)
-
-    def do_copy(k):
-        return rc(do_ref, do_all.at[own_c, :], do_ss.at[k - 1], do_rs.at[k - 1], cdev(k))
-
-    for k in (2, 1, 3):
-        do_copy(k).start()
-    do_all[own_c, :] = do_ref[...]
 
     @pl.loop(0, NB)
     def _(j):
@@ -141,24 +135,67 @@
         h = g * jax.nn.sigmoid(g) * up_ref[:, cols].astype(F32)
         ht_all[cols, own_r] = h.T.astype(BF)
 
-    def ht_copy(i, k):
+    pl.semaphore_wait(barrier, len(partners))
+
+    c_far = lax.rem(c + 2, 4)
+    c_near = c + 1 - 2 * lax.rem(c, 2)
+    far_dev, near_dev = (d, r, c_far), (d, r, c_near)
+
+    def do_copy(n):
+        rows = own_c if n < 2 else rows_of(c_far, 128)
+        view = do_all.at[rows, :]
+        return rc(do_ref if n < 2 else view, view, do_ss.at[n], do_rs.at[n],
+                  near_dev if n else far_dev)
+
+    for n in range(2):
+        do_copy(n).start()
+    do_all[own_c, :] = do_ref[...]
+
+    def row_dev(n):
+        return ydev(3 if n % 2 else 1)
+
+    def row_block(n):
+        return rows_of(r if n < 2 else lax.rem(r + (1 if n % 2 else 3), 4), 128)
+
+    def ht_copy(i, n):
         away = (2 * lax.rem(i, 2) - 1) * (4 - lax.div(i + 1, 2))
-        view = ht_all.at[rows_of(zmod(z + away), UR), own_r]
-        return rc(view, view, ht_ss.at[i, k - 1], ht_rs.at[i, k - 1], ydev(k))
-
-    @pl.loop(0, NZ)
-    def _(i):
-        for k in (2, 1, 3):
-            ht_copy(i, k).start()
+        first = zmod(z + away) * UR
+        if n < 2:
+            rows = pl.ds(pl.multiple_of(first, 64), UR)
+        else:
+            rows = pl.ds(pl.multiple_of(first + (n - 2) * 224, 32), 224)
+        view = ht_all.at[rows, row_block(n)]
+        return rc(view, view, ht_ss.at[i, n], ht_rs.at[i, n], row_dev(n))
+
+    def ht_send(first, last):
+        @pl.loop(first, last)
+        def _(i):
+            for n in range(2):
+                ht_copy(i, n).start()
+
+    def ht_pass(first, last):
+        @pl.loop(first, last)
+        def _(i):
+            for n in range(2):
+                ht_copy(i, n).wait_recv()
+                ht_copy(i, n + 2).start()
+
+    def ht_wait(first, last):
+        @pl.loop(first, last)
+        def _(i):
+            for n in (2, 3):
+                ht_copy(i, n).wait_recv()
+
+    ht_send(0, 3)
 
     xt_all[:, own_c] = x_ref[...].T
 
-    def xt_copy(k):
-        view = xt_all.at[:, own_c]
-        return rc(view, view, xt_ss.at[k - 1], xt_rs.at[k - 1], cdev(k))
-
-    for k in (2, 1, 3):
-        xt_copy(k).start()
+    def xt_copy(n):
+        view = xt_all.at[:, own_c if n < 2 else rows_of(c_far, 128)]
+        return rc(view, view, xt_ss.at[n], xt_rs.at[n], near_dev if n else far_dev)
+
+    for n in range(2):
+        xt_copy(n).start()
 
     def a_copy(j, par, k):
         return rc(a_s.at[par, k - 1], a_r.at[j, k - 1], a_ss.at[par, k - 1],
@@ -185,9 +222,19 @@
         def _():
             wd_copy(j + 2, par).start()
 
-    def b_copy(q, k):
-        view = gu.at[q, own_r, :]
-        return rc(view, view, b_ss.at[q, k - 1], b_rs.at[q, k - 1], ydev(k))
+    def b_copy(q, n):
+        if n < 2:
+            view = gu.at[q, row_block(n), :]
+        else:
+            first = lax.rem(r + (1 if n % 2 else 3), 4) * 128 + (n - 2) * 64
+            view = gu.at[q, pl.ds(pl.multiple_of(first, 64), 64), :]
+        return rc(view, view, b_ss.at[q, n], b_rs.at[q, n], row_dev(n))
+
+    def pass_b(j):
+        for t in range(2):
+            for n in range(2):
+                b_copy(2 * j + t, n).wait_recv()
+                b_copy(2 * j + t, n + 2).start()
 
     def stage_b(j):
         par = lax.rem(j, 2)
@@ -209,8 +256,8 @@
             gu[2 * j + 1, dst, :] = (hg * (g * sig)).astype(BF)
 
         for t in range(2):
-            for k in (2, 1, 3):
-                b_copy(2 * j + t, k).start()
+            for n in range(2):
+                b_copy(2 * j + t, n).start()
 
     def ring(step, job, par, sign, first, slots, ssem, rsem, hops, dot):
         dest = zmod(z + sign * (hops - step))
@@ -243,25 +290,64 @@
     own_u = rows_of(xl, 224)
     other_u = rows_of(1 - xl, 224)
 
+    def half_dot(k, dest, side):
+        rows = pl.ds(pl.multiple_of(dest * UR + side * 224, 32), 224)
+        return dot_nn(ht_all[rows, :], do_all[:, rows_of(k + DK, DC)])
+
+    def dxp_copy(k, dest):
+        return rc(xpsd.at[k, dest], xprd.at[k, dest], dxp_ss.at[k, dest], dxp_rs.at[k, dest], xdev)
+
+    def downx_pre(step):
+        @pl.loop(0, DK)
+        def _(k):
+            sign = 1 - 2 * k
+            dests = [zmod(z + sign * (4 - step))]
+            if step < 3:
+                dests.append(zmod(z - sign * (3 - step)))
+            for dest in dests:
+                xpsd[k, dest] = half_dot(k, dest, 1 - xl).astype(BF)
+                dxp_copy(k, dest).start()
+
+    def downx_dot(k):
+        def dot(dest):
+            val = half_dot(k, dest, xl)
+            dxp_copy(k, dest).wait()
+            return val + xprd[k, dest].astype(F32)
+        return dot
+
     def dx_copy(k):
         return rc(xsd.at[k], xrd.at[k], dx_ss.at[k], dx_rs.at[k], xdev)
 
     def down_step(step):
         @pl.loop(0, DK)
         def _(k):
-            sign = 1 - 2 * lax.rem(k, 2)
+            sign = 1 - 2 * k
             ring(step, k, k, sign, s0d.at[0], rld, dl_ss, dl_rs, 4, down_dot(k))
             if step < 3:
                 ring(step, k, k, -sign, s0d.at[1], rsd, dh_ss, dh_rs, 3, down_dot(k))
 
+    def downx_step(step):
+        @pl.loop(0, DK)
+        def _(k):
+            sign = 1 - 2 * k
+            ring(step, k, k, sign, s0dx.at[0], rldx, dlx_ss, dlx_rs, 4, downx_dot(k))
+            if step < 3:
+                ring(step, k, k, -sign, s0dx.at[1], rsdx, dhx_ss, dhx_rs, 3, downx_dot(k))
+
     def down_end():
         @pl.loop(0, DK)
         def _(k):
-            sign = 1 - 2 * lax.rem(k, 2)
+            sign = 1 - 2 * k
             find[...] = ring_end(k, k, sign, rld, rsd, dl_ss, dl_rs, dh_ss, dh_rs, down_dot(k))
-            accd[k] = find[own_u, :]
             xsd[k] = find[other_u, :].astype(BF)
             dx_copy(k).start()
+            accd[k] = find[own_u, :]
+
+        @pl.loop(0, DK)
+        def _(k):
+            sign = 1 - 2 * k
+            accd[k + DK] = ring_end(
+                k, k, sign, rldx, rsdx, dlx_ss, dlx_rs, dhx_ss, dhx_rs, downx_dot(k))
 
     def da_out(i):
         return lc(dab.at[i], (nd, ndm, ndv)[i], da_sem.at[i])
@@ -274,86 +360,128 @@
         @pl.loop(0, DK)
         def _(k):
             dx_copy(k).wait()
+            accd[k] += xrd[k].astype(F32)
+
+        @pl.loop(0, 2 * DK)
+        def _(k):
             cols = rows_of(k, DC)
 
             @pl.loop(0, 7)
             def _(i):
                 sub = rows_of(i, 32)
-                grad = accd[k, sub, :] + xrd[k, sub, :].astype(F32)
-                new = adamw(dab[0, sub, cols], dab[1, sub, cols], dab[2, sub, cols], grad)
+                new = adamw(
+                    dab[0, sub, cols], dab[1, sub, cols], dab[2, sub, cols], accd[k, sub, :])
                 for n in range(3):
                     dab[n, sub, cols] = new[n]
 
         for i in range(3):
             da_out(i).start()
 
-    def gu_dot(q):
+    def gate_dot(j):
         def dot(dest):
-            return dot_nn(xt_all[rows_of(dest, ZR), :], gu[q])
+            return dot_nn(xt_all[rows_of(dest, ZR), :], gu[2 * j])
         return dot
 
     own_w = rows_of(xl, 64)
     other_w = rows_of(1 - xl, 64)
 
-    def x_copy(q):
-        par = lax.rem(q, 2)
-        return rc(xs.at[par], xr.at[q], x_ss.at[par], x_rs.at[q], xdev)
-
-    def ab_copies(q, par, out):
-        cols = rows_of(lax.div(q, 2), CB)
-        for t in range(2):
-            refs = ((ng, ngm, ngv), (nu, num, nuv))[t] if out else ((wg, gm, gv), (wu, um, uv))[t]
-
-            @pl.when(par == t)
+    def up_half(j, dest, side):
+        rows = pl.ds(pl.multiple_of(dest * ZR + side * 64, 64), 64)
+        return dot_nn(xt_all[rows, :], gu[2 * j + 1])
+
+    def xp_copy(j, dest):
+        par = lax.rem(j, 2)
+        return rc(xps.at[par, dest], xpr.at[j, dest], xp_ss.at[par, dest], xp_rs.at[j, dest], xdev)
+
+    def up_pre(j):
+        par = lax.rem(j, 2)
+        sign = 2 * par - 1
+
+        @pl.loop(0, NZ)
+        def _(i):
+            away = sign * (1 - 2 * lax.rem(i, 2)) * (4 - lax.div(i + 1, 2))
+            dest = zmod(z + away)
+
+            @pl.when(j >= 2)
             def _():
-                for n in range(3):
-                    if out:
-                        lc(abuf.at[t, n], refs[n].at[:, cols], ob_sem.at[t, n]).start()
-                    elif n == 0:
-                        lc(refs[0].at[rows_of(d, 64), cols], abuf.at[t, n], ab_sem.at[t, n]).start()
-                    else:
-                        lc(refs[n].at[:, cols], abuf.at[t, n], ab_sem.at[t, n]).start()
-
-    def ob_wait(par):
+                xp_copy(j, dest).wait_send()
+
+            xps[par, dest] = up_half(j, dest, 1 - xl).astype(BF)
+            xp_copy(j, dest).start()
+
+    def up_dot(j):
+        def dot(dest):
+            val = up_half(j, dest, xl)
+            xp_copy(j, dest).wait_recv()
+            return val + xpr[j, dest].astype(F32)
+        return dot
+
+    def x_copy(j):
+        par = lax.rem(j, 2)
+        return rc(xs.at[par], xr.at[j], x_ss.at[par], x_rs.at[j], xdev)
+
+    def ab_in(t, j):
+        @pl.when(j >= 1)
+        def _():
+            ob_wait(t)
+
+        cols = rows_of(j, CB)
+        w, m, v = ((wg, gm, gv), (wu, um, uv))[t]
+        lc(w.at[rows_of(d, 64), cols], abuf.at[t, 0], ab_sem.at[t, 0]).start()
+        lc(m.at[:, cols], abuf.at[t, 1], ab_sem.at[t, 1]).start()
+        lc(v.at[:, cols], abuf.at[t, 2], ab_sem.at[t, 2]).start()
+
+    def ob_wait(t):
         for n in range(3):
-            lc(abuf.at[par, n], ng.at[:, pl.ds(0, CB)], ob_sem.at[par, n]).wait()
-
-    def gu_step(step, q):
-        par = lax.rem(q, 2)
+            lc(abuf.at[t, n], ng.at[:, pl.ds(0, CB)], ob_sem.at[t, n]).wait()
+
+    def gate_step(step, j):
+        par = lax.rem(j, 2)
         sign = 1 - 2 * par
-        ring(step, q, par, sign, s0.at[0], rl, l_ss, l_rs, 4, gu_dot(q))
+        ring(step, j, par, sign, s0.at[0], rl, l_ss, l_rs, 4, gate_dot(j))
         if step < 3:
-            ring(step, q, par, -sign, s0.at[1], rs, h_ss, h_rs, 3, gu_dot(q))
-
-    def gu_end(q):
-        par = lax.rem(q, 2)
-
-        @pl.when(q >= 2)
-        def _():
-            ob_wait(par)
-
-        ab_copies(q, par, False)
-        sign = 1 - 2 * par
-        fin[...] = ring_end(q, par, sign, rl, rs, l_ss, l_rs, h_ss, h_rs, gu_dot(q))
+            ring(step, j, par, -sign, s0.at[1], rs, h_ss, h_rs, 3, gate_dot(j))
+
+    def up_step(step, j):
+        par = lax.rem(j, 2)
+        sign = 2 * par - 1
+        ring(step, j, par, sign, s0x.at[0], rlx, lx_ss, lx_rs, 4, up_dot(j))
+        if step < 3:
+            ring(step, j, par, -sign, s0x.at[1], rsx, hx_ss, hx_rs, 3, up_dot(j))
+
+    def gate_end(j):
+        par = lax.rem(j, 2)
+        fin[...] = ring_end(j, par, 1 - 2 * par, rl, rs, l_ss, l_rs, h_ss, h_rs, gate_dot(j))
         xs[par] = fin[other_w, :].astype(BF)
-        x_copy(q).start()
+        x_copy(j).start()
         acc[par] = fin[own_w, :]
 
-    def gu_update(q):
-        par = lax.rem(q, 2)
+    def up_end(j):
+        par = lax.rem(j, 2)
+        acc[2] = ring_end(j, par, 2 * par - 1, rlx, rsx, lx_ss, lx_rs, hx_ss, hx_rs, up_dot(j))
+        update(1, j, 2)
+
+    def gate_update(j):
+        x_copy(j).wait()
+        par = lax.rem(j, 2)
+        acc[par] += xr[j].astype(F32)
+        update(0, j, par)
+
+    def update(t, j, slot):
         for n in range(3):
-            lc(gm.at[:, pl.ds(0, CB)], abuf.at[par, n], ab_sem.at[par, n]).wait()
-        x_copy(q).wait()
+            lc(gm.at[:, pl.ds(0, CB)], abuf.at[t, n], ab_sem.at[t, n]).wait()
 
         @pl.loop(0, 4)
         def _(i):
             sub = rows_of(i, 16)
-            grad = acc[par, sub, :] + xr[q, sub, :].astype(F32)
-            new = adamw(abuf[par, 0, sub, :], abuf[par, 1, sub, :], abuf[par, 2, sub, :], grad)
+            new = adamw(abuf[t, 0, sub, :], abuf[t, 1, sub, :], abuf[t, 2, sub, :], acc[slot, sub, :])
             for n in range(3):
-                abuf[par, n, sub, :] = new[n]
-
-        ab_copies(q, par, True)
+                abuf[t, n, sub, :] = new[n]
+
+        cols = rows_of(j, CB)
+        refs = ((ng, ngm, ngv), (nu, num, nuv))[t]
+        for n in range(3):
+            lc(abuf.at[t, n], refs[n].at[:, cols], ob_sem.at[t, n]).start()
 
     def ig_add(q):
         par = lax.rem(q, 2)
@@ -393,60 +521,105 @@
         igo[...] = val.astype(BF)
         lc(igo, ig_out, igo_sem).start()
 
-    def ht_wait(*blocks):
-        for i in blocks:
-            for k in (2, 1, 3):
-                ht_copy(i, k).wait_recv()
-
-    for k in (2, 1, 3):
-        do_copy(k).wait()
-
-    @pl.loop(0, 4)
-    def _(i):
-        stage_a(i)
-
-        @pl.when(i >= 1)
-        def _():
-            stage_b(i - 1)
-
-        for step, blocks in enumerate(((0, 1, 2), (3, 4), (5, 6), (7,))):
-            @pl.when(i == step)
-            def _():
-                ht_wait(*blocks)
-                down_step(step)
-
-    for k in (2, 1, 3):
-        xt_copy(k).wait()
-
-    @pl.loop(0, NQ + 5)
+    def relayed(copy):
+        copy(0).wait_recv()
+        copy(2).start()
+        copy(0).wait_send()
+        copy(1).wait()
+        copy(2).wait()
+
+    ht_pass(0, 3)
+    relayed(do_copy)
+    stage_a(0)
+    ht_send(3, 5)
+    ht_wait(0, 3)
+    downx_pre(0)
+    down_step(0)
+    downx_step(0)
+
+    ht_pass(3, 5)
+    stage_a(1)
+    ht_send(5, 7)
+    ht_wait(3, 5)
+    downx_pre(1)
+    down_step(1)
+    downx_step(1)
+
+    ht_pass(5, 7)
+    stage_b(0)
+    ht_send(7, 8)
+    ht_wait(5, 7)
+    downx_pre(2)
+    down_step(2)
+    downx_step(2)
+
+    stage_a(2)
+    ht_pass(7, 8)
+    pass_b(0)
+    stage_b(1)
+    ht_wait(7, 8)
+    downx_pre(3)
+    downx_pre(4)
+    down_step(3)
+    downx_step(3)
+    relayed(xt_copy)
+
+    def up_gate_ready(q):
+        for n in (2, 3):
+            b_copy(q, n).wait_recv()
+
+    @pl.loop(0, NQ + 4)
     def _(t):
         for step in (3, 2, 1, 0):
             q = t - step
-
-            @pl.when((q >= 0) & (q < NQ))
+            job = lax.div(q, 2)
+
+            @pl.when((q >= 0) & (q < NQ) & (lax.rem(q, 2) == 0))
             def _():
                 if step == 0:
-                    for k in (2, 1, 3):
-                        b_copy(q, k).wait_recv()
-                gu_step(step, q)
+                    up_gate_ready(q)
+                gate_step(step, job)
+
+            @pl.when((q >= 0) & (q < NQ) & (lax.rem(q, 2) == 1))
+            def _():
+                if step == 3:
+                    ab_in(1, job)
+                up_step(step, job)
+
+        @pl.when((t < NQ) & (lax.rem(t, 2) == 0))
+        def _():
+            up_gate_ready(t + 1)
+            up_pre(lax.div(t, 2))
 
         half = lax.div(t, 2)
 
-        @pl.when((lax.rem(t, 2) == 0) & (half + 4 < NB))
-        def _():
-            stage_a(half + 4)
-
-        @pl.when((lax.rem(t, 2) == 1) & (half + 3 < NB))
-        def _():
-            stage_b(half + 3)
-
-        @pl.when((t >= 4) & (t - 4 < NQ))
-        def _():
-            gu_end(t - 4)
-
-        @pl.when(t >= 5)
-        def _():
-            gu_update(t - 5)
+        @pl.when((lax.rem(t, 2) == 0) & (half + 1 < NB))
+        def _():
+            pass_b(half + 1)
+
+        @pl.when((lax.rem(t, 2) == 0) & (half + 3 < NB))
+        def _():
+            stage_a(half + 3)
+
+        @pl.when((lax.rem(t, 2) == 1) & (half + 2 < NB))
+        def _():
+            stage_b(half + 2)
+
+        @pl.when((t >= 4) & (lax.rem(t, 2) == 0))
+        def _():
+            gate_end(lax.div(t - 4, 2))
+
+        @pl.when((t >= 5) & (lax.rem(t, 2) == 1))
+        def _():
+            up_end(lax.div(t - 5, 2))
+
+        @pl.when((t >= 7) & (lax.rem(t, 2) == 1))
+        def _():
+            gate_update(lax.div(t - 7, 2))
+
+        @pl.when((t >= 5) & (lax.rem(t, 2) == 1))
+        def _():
+            ab_in(0, lax.div(t - 5, 2))
 
         @pl.when(t < NQ)
         def _():
@@ -464,10 +637,8 @@
         def _():
             ig_send()
 
-        @pl.when(t == NQ + 3)
-        def _():
-            ig_end()
-
+    gate_update(NB - 1)
+    ig_end()
     for i in range(3):
         da_out(i).wait()
     lc(igo, ig_out, igo_sem).wait()
@@ -478,13 +649,31 @@
 
     @pl.loop(0, NZ)
     def _(i):
-        for k in (2, 1, 3):
-            ht_copy(i, k).wait_send()
+        for n in range(4):
+            ht_copy(i, n).wait_send()
 
     @pl.loop(0, NQ)
     def _(q):
-        for k in (2, 1, 3):
-            b_copy(q, k).wait_send()
+        for n in range(4):
+            b_copy(q, n).wait_send()
+
+    @pl.loop(0, NZ)
+    def _(i):
+        for j in (NB - 2, NB - 1):
+            xp_copy(j, i).wait_send()
+
+
+def hand_over(*refs):
+    src, dst, buf = refs[:10], refs[10:20], refs[20:30]
+    ins = [pltpu.make_async_copy(src[i], buf[i], refs[30].at[i]) for i in range(10)]
+    outs = [pltpu.make_async_copy(buf[i], dst[i], refs[31].at[i]) for i in range(10)]
+    for copy in ins:
+        copy.start()
+    for i in range(10):
+        ins[i].wait()
+        outs[i].start()
+    for copy in outs:
+        copy.wait()
 
 
 def on_device(*args):
@@ -501,44 +690,57 @@
         vm((2, 128, CB), F32),
         vm((NB, 3, 128, CB), BF),
         vm((2, 2, ZR, CB), BF),
-        vm((NQ, 4, ZR, CB), BF),
-        vm((NQ, 3, ZR, CB), BF),
+        vm((NB, 4, ZR, CB), BF),
+        vm((NB, 3, ZR, CB), BF),
         vm((ZR, CB), F32),
-        vm((2, 64, CB), F32),
+        vm((3, 64, CB), F32),
         vm((2, 64, CB), BF),
-        vm((NQ, 64, CB), BF),
+        vm((NB, 64, CB), BF),
         vm((2, 3, 64, CB), BF),
+        vm((2, 2, 64, CB), BF),
+        vm((NB, 4, 64, CB), BF),
+        vm((NB, 3, 64, CB), BF),
+        vm((2, NZ, 64, CB), BF),
+        vm((NB, NZ, 64, CB), BF),
         vm((2, DK, UR, DC), BF),
         vm((DK, 4, UR, DC), BF),
         vm((DK, 3, UR, DC), BF),
         vm((UR, DC), F32),
-        vm((DK, 224, DC), F32),
+        vm((2 * DK, 224, DC), F32),
         vm((DK, 224, DC), BF),
         vm((DK, 224, DC), BF),
         vm((3, 224, 1024), BF),
+        vm((2, DK, 224, DC), BF),
+        vm((DK, 4, 224, DC), BF),
+        vm((DK, 3, 224, DC), BF),
+        vm((DK, NZ, 224, DC), BF),
+        vm((DK, NZ, 224, DC), BF),
         vm((512, 1024), F32),
         vm((3, 128, 1024), BF),
         vm((3, 128, 1024), BF),
         vm((128, 1024), BF),
         dma((3,)), dma((3,)), dma((3,)), dma((3,)),
-        dma((NZ, 3)), dma((NZ, 3)),
+        dma((NZ, 4)), dma((NZ, 4)),
         dma((2, 3)), dma((NB, 3)),
-        dma((NQ, 3)), dma((NQ, 3)),
-        dma((2, 4)), dma((NQ, 4)),
-        dma((2, 3)), dma((NQ, 3)),
-        dma((2,)), dma((NQ,)),
-        dma((DK, 4)), dma((DK, 4)),
-        dma((DK, 3)), dma((DK, 3)),
+        dma((NQ, 4)), dma((NQ, 4)),
+        dma((2, 4)), dma((NB, 4)), dma((2, 3)), dma((NB, 3)),
+        dma((2,)), dma((NB,)),
+        dma((2, 4)), dma((NB, 4)), dma((2, 3)), dma((NB, 3)),
+        dma((2, NZ)), dma((NB, NZ)),
+        dma((DK, 4)), dma((DK, 4)), dma((DK, 3)), dma((DK, 3)),
         dma((DK,)), dma((DK,)),
+        dma((DK, 4)), dma((DK, 4)), dma((DK, 3)), dma((DK, 3)),
+        dma((DK, NZ)), dma((DK, NZ)),
         dma((3,)), dma((3,)),
         dma((2,)), dma((2,)), dma((2, 3)), dma((2, 3)), dma((3,)), dma(()),
     ]
     shapes = [(128, 1024)] + [(64, 3584)] * 6 + [(224, 1024)] * 3
     in_vmem = pl.BlockSpec(memory_space=pltpu.VMEM)
     in_any = pl.BlockSpec(memory_space=pl.ANY)
-    return pl.pallas_call(
+    shapes = [jax.ShapeDtypeStruct(s, BF) for s in shapes]
+    results = pl.pallas_call(
         kernel,
-        out_shape=[jax.ShapeDtypeStruct(s, BF) for s in shapes],
+        out_shape=shapes,
         in_specs=[in_vmem] * 4 + [in_any] * 9,
         out_specs=[in_any] * 10,
         scratch_shapes=scratch,
@@ -549,6 +751,13 @@
             flops=22548578304, bytes_accessed=34000000, transcendentals=4000000
         ),
     )(*args)
+    return pl.pallas_call(
+        hand_over,
+        out_shape=shapes,
+        in_specs=[in_any] * 10,
+        out_specs=[in_any] * 10,
+        scratch_shapes=[vm(s.shape, BF) for s in shapes] + [dma((10,)), dma((10,))],
+    )(*results)
 
 
 def solution(mesh):

time: 281 us -> 228 us (0.81)
  Pallas kernels: 259 us -> 225 us
  local copies, waits for them, and re-layouts: 17 us -> 0 us
    pallas_call x1 -> x2, Pallas kernels: 259 us -> 225 us  [the longest x1 221 us: on_device(): pl.pallas_call(kernel, out_shape=shapes, in_specs=[in_vmem] * 4 + [in_any...]
    unnamed x12 -> x0, local copies, waits for them, and re-layouts: 17 us -> none
where the time goes in v2:
time: 228 us; the launch traced here: 226 us
  Pallas kernels  225 us (99%)
    pallas_call x1, Pallas kernels, on_device(): pl.pallas_call(kernel, out_shape=shapes, in_specs=[in_vmem] * 4 + [in_any...  221 us

profile of v2, /device:TPU:1, one launch (start us, length us, event | category | flops | bytes accessed | tf_op | source)
XLA Modules:
  0.0 225.8 jit_solution(6968231180795030800)
XLA Ops:
  0.6 221.0 %shard_map.204 = (bf16[128,1024]{1,0:T(8,128)(2,1)}, bf16[64,3584]{1,0:T(8,128)(2,1)}, bf16[64,3584]{1,0:T(8,128)(2,1)}, bf16[64,3584]{1,0:T(8,128)(2,1)}, bf16[...) custom-call(bf16[128,1024]{1,0:T(8,128)(2,1)} %x_ref.1, ...), custom_call_target="tpu_custom_call" | custom-call | flops 22548578304 | bytes 34000000 | tf_op jit(solution)/shard_map/pallas_call | solution.py:741
  221.6 4.0 %shard_map.205 = (bf16[128,1024]{1,0:T(8,128)(2,1)}, bf16[64,3584]{1,0:T(8,128)(2,1)}, bf16[64,3584]{1,0:T(8,128)(2,1)}, bf16[64,3584]{1,0:T(8,128)(2,1)}, bf16[...) custom-call(bf16[128,1024]{1,0:T(8,128)(2,1)} %get-tuple-element.20., ...), custom_call_target="tpu_custom_call" | custom-call | tf_op jit(solution)/shard_map/pallas_call | solution.py:754

commit v3 on v2

--- a/solution.py
+++ b/solution.py
@@ -194,9 +194,6 @@
         view = xt_all.at[:, own_c if n < 2 else rows_of(c_far, 128)]
         return rc(view, view, xt_ss.at[n], xt_rs.at[n], near_dev if n else far_dev)
 
-    for n in range(2):
-        xt_copy(n).start()
-
     def a_copy(j, par, k):
         return rc(a_s.at[par, k - 1], a_r.at[j, k - 1], a_ss.at[par, k - 1],
                   a_rs.at[j, k - 1], ydev(k))
@@ -297,12 +294,14 @@
     def dxp_copy(k, dest):
         return rc(xpsd.at[k, dest], xprd.at[k, dest], dxp_ss.at[k, dest], dxp_rs.at[k, dest], xdev)
 
-    def downx_pre(step):
+    def downx_pre(step, ways="lh"):
         @pl.loop(0, DK)
         def _(k):
             sign = 1 - 2 * k
-            dests = [zmod(z + sign * (4 - step))]
-            if step < 3:
+            dests = []
+            if "l" in ways:
+                dests.append(zmod(z + sign * (4 - step)))
+            if "h" in ways and step < 3:
                 dests.append(zmod(z - sign * (3 - step)))
             for dest in dests:
                 xpsd[k, dest] = half_dot(k, dest, 1 - xl).astype(BF)
@@ -318,20 +317,22 @@
     def dx_copy(k):
         return rc(xsd.at[k], xrd.at[k], dx_ss.at[k], dx_rs.at[k], xdev)
 
-    def down_step(step):
+    def down_step(step, ways="lh"):
         @pl.loop(0, DK)
         def _(k):
             sign = 1 - 2 * k
-            ring(step, k, k, sign, s0d.at[0], rld, dl_ss, dl_rs, 4, down_dot(k))
-            if step < 3:
+            if "l" in ways:
+                ring(step, k, k, sign, s0d.at[0], rld, dl_ss, dl_rs, 4, down_dot(k))
+            if "h" in ways and step < 3:
                 ring(step, k, k, -sign, s0d.at[1], rsd, dh_ss, dh_rs, 3, down_dot(k))
 
-    def downx_step(step):
+    def downx_step(step, ways="lh"):
         @pl.loop(0, DK)
         def _(k):
             sign = 1 - 2 * k
-            ring(step, k, k, sign, s0dx.at[0], rldx, dlx_ss, dlx_rs, 4, downx_dot(k))
-            if step < 3:
+            if "l" in ways:
+                ring(step, k, k, sign, s0dx.at[0], rldx, dlx_ss, dlx_rs, 4, downx_dot(k))
+            if "h" in ways and step < 3:
                 ring(step, k, k, -sign, s0dx.at[1], rsdx, dhx_ss, dhx_rs, 3, downx_dot(k))
 
     def down_end():
@@ -530,38 +531,42 @@
 
     ht_pass(0, 3)
     relayed(do_copy)
-    stage_a(0)
     ht_send(3, 5)
-    ht_wait(0, 3)
-    downx_pre(0)
-    down_step(0)
-    downx_step(0)
+    ht_wait(0, 1)
+    down_step(0, "l")
+    downx_pre(0, "l")
+    ht_wait(1, 3)
+    down_step(0, "h")
+    downx_pre(0, "h")
 
     ht_pass(3, 5)
-    stage_a(1)
     ht_send(5, 7)
     ht_wait(3, 5)
+    down_step(1)
     downx_pre(1)
-    down_step(1)
+    ht_pass(5, 7)
+    ht_send(7, 8)
+    stage_a(0)
+    downx_step(0)
+
+    ht_wait(5, 7)
+    down_step(2)
+    downx_pre(2)
+    for n in range(2):
+        xt_copy(n).start()
+    ht_pass(7, 8)
+    stage_a(1)
     downx_step(1)
-
-    ht_pass(5, 7)
     stage_b(0)
-    ht_send(7, 8)
-    ht_wait(5, 7)
-    downx_pre(2)
-    down_step(2)
+
+    ht_wait(7, 8)
+    down_step(3)
+    downx_pre(3)
+    downx_pre(4)
+    stage_a(2)
     downx_step(2)
-
-    stage_a(2)
-    ht_pass(7, 8)
     pass_b(0)
     stage_b(1)
-    ht_wait(7, 8)
-    downx_pre(3)
-    downx_pre(4)
-    down_step(3)
-    downx_step(3)
     relayed(xt_copy)
 
     def up_gate_ready(q):
@@ -625,11 +630,15 @@
         def _():
             ig_add(t)
 
-        @pl.when(t == 1)
+        @pl.when(t == 0)
+        def _():
+            downx_step(3)
+
+        @pl.when(t == 2)
         def _():
             down_end()
 
-        @pl.when(t == 2)
+        @pl.when(t == 3)
         def _():
             down_update()
 

time: 228 us -> 216 us (0.947)
  Pallas kernels: 225 us -> 214 us
    pallas_call x1, Pallas kernels: 221 us -> 210 us  [on_device(): pl.pallas_call(kernel, out_shape=shapes, in_specs=[in_vmem] * 4 + [in_any...]
where the time goes in v3:
time: 216 us; the launch traced here: 215 us
  Pallas kernels  214 us (99%)
    pallas_call x1, Pallas kernels, on_device(): pl.pallas_call(kernel, out_shape=shapes, in_specs=[in_vmem] * 4 + [in_any...  210 us

profile of v3, /device:TPU:1, one launch (start us, length us, event | category | flops | bytes accessed | tf_op | source)
XLA Modules:
  0.0 215.3 jit_solution(6964393712884164307)
XLA Ops:
  0.6 210.4 %shard_map.204 = (bf16[128,1024]{1,0:T(8,128)(2,1)}, bf16[64,3584]{1,0:T(8,128)(2,1)}, bf16[64,3584]{1,0:T(8,128)(2,1)}, bf16[64,3584]{1,0:T(8,128)(2,1)}, bf16[...) custom-call(bf16[128,1024]{1,0:T(8,128)(2,1)} %x_ref.1, ...), custom_call_target="tpu_custom_call" | custom-call | flops 22548578304 | bytes 34000000 | tf_op jit(solution)/shard_map/pallas_call | solution.py:750
  211.1 4.0 %shard_map.205 = (bf16[128,1024]{1,0:T(8,128)(2,1)}, bf16[64,3584]{1,0:T(8,128)(2,1)}, bf16[64,3584]{1,0:T(8,128)(2,1)}, bf16[64,3584]{1,0:T(8,128)(2,1)}, bf16[...) custom-call(bf16[128,1024]{1,0:T(8,128)(2,1)} %get-tuple-element.20., ...), custom_call_target="tpu_custom_call" | custom-call | tf_op jit(solution)/shard_map/pallas_call | solution.py:763

commit v4 on v3

--- a/solution.py
+++ b/solution.py
@@ -598,41 +598,41 @@
 
         half = lax.div(t, 2)
 
+        @pl.when((lax.rem(t, 2) == 0) & (half + 3 < NB))
+        def _():
+            stage_a(half + 3)
+
+        @pl.when((lax.rem(t, 2) == 1) & (half + 2 < NB))
+        def _():
+            stage_b(half + 2)
+
+        @pl.when((t >= 4) & (lax.rem(t, 2) == 0))
+        def _():
+            gate_end(lax.div(t - 4, 2))
+
+        @pl.when((t >= 5) & (lax.rem(t, 2) == 1))
+        def _():
+            up_end(lax.div(t - 5, 2))
+
+        @pl.when((t >= 7) & (lax.rem(t, 2) == 1))
+        def _():
+            gate_update(lax.div(t - 7, 2))
+
+        @pl.when((t >= 5) & (lax.rem(t, 2) == 1))
+        def _():
+            ab_in(0, lax.div(t - 5, 2))
+
+        @pl.when(t < NQ)
+        def _():
+            ig_add(t)
+
+        @pl.when(t == 0)
+        def _():
+            downx_step(3)
+
         @pl.when((lax.rem(t, 2) == 0) & (half + 1 < NB))
         def _():
             pass_b(half + 1)
-
-        @pl.when((lax.rem(t, 2) == 0) & (half + 3 < NB))
-        def _():
-            stage_a(half + 3)
-
-        @pl.when((lax.rem(t, 2) == 1) & (half + 2 < NB))
-        def _():
-            stage_b(half + 2)
-
-        @pl.when((t >= 4) & (lax.rem(t, 2) == 0))
-        def _():
-            gate_end(lax.div(t - 4, 2))
-
-        @pl.when((t >= 5) & (lax.rem(t, 2) == 1))
-        def _():
-            up_end(lax.div(t - 5, 2))
-
-        @pl.when((t >= 7) & (lax.rem(t, 2) == 1))
-        def _():
-            gate_update(lax.div(t - 7, 2))
-
-        @pl.when((t >= 5) & (lax.rem(t, 2) == 1))
-        def _():
-            ab_in(0, lax.div(t - 5, 2))
-
-        @pl.when(t < NQ)
-        def _():
-            ig_add(t)
-
-        @pl.when(t == 0)
-        def _():
-            downx_step(3)
 
         @pl.when(t == 2)
         def _():

time: 216 us -> 212 us (0.981); the launches traced: 215 us -> 209 us
  Pallas kernels: 214 us -> 208 us
    pallas_call x1, Pallas kernels: 210 us -> 204 us  [on_device(): pl.pallas_call(kernel, out_shape=shapes, in_specs=[in_vmem] * 4 + [in_any...]
where the time goes in v4:
time: 212 us; the launch traced here: 209 us
  Pallas kernels  208 us (98%)
    pallas_call x1, Pallas kernels, on_device(): pl.pallas_call(kernel, out_shape=shapes, in_specs=[in_vmem] * 4 + [in_any...  204 us

profile of v4, /device:TPU:1, one launch (start us, length us, event | category | flops | bytes accessed | tf_op | source)
XLA Modules:
  0.0 208.8 jit_solution(11774054603677562174)
XLA Ops:
  0.6 204.0 %shard_map.204 = (bf16[128,1024]{1,0:T(8,128)(2,1)}, bf16[64,3584]{1,0:T(8,128)(2,1)}, bf16[64,3584]{1,0:T(8,128)(2,1)}, bf16[64,3584]{1,0:T(8,128)(2,1)}, bf16[...) custom-call(bf16[128,1024]{1,0:T(8,128)(2,1)} %x_ref.1, ...), custom_call_target="tpu_custom_call" | custom-call | flops 22548578304 | bytes 34000000 | tf_op jit(solution)/shard_map/pallas_call | solution.py:750
  204.6 4.0 %shard_map.205 = (bf16[128,1024]{1,0:T(8,128)(2,1)}, bf16[64,3584]{1,0:T(8,128)(2,1)}, bf16[64,3584]{1,0:T(8,128)(2,1)}, bf16[64,3584]{1,0:T(8,128)(2,1)}, bf16[...) custom-call(bf16[128,1024]{1,0:T(8,128)(2,1)} %get-tuple-element.20., ...), custom_call_target="tpu_custom_call" | custom-call | tf_op jit(solution)/shard_map/pallas_call | solution.py:763
